TPU v7x, 512 devices: a whole 4x8x8 slice. The times are simulated.
512 devices in a mesh: tm: 16 (over y, core), space: 32 (over x, z).
Axes of the slice: x: 4, y: 8, z: 8, core: 2. Of those that a mesh axis runs over, the one named last changes fastest.
Arguments:
- coupling: bfloat16 [16, 2048, 2048], P('tm', 'space'), may hold values from -0.125 to 0.125
- arrow_link: float32 [16, 2048, 64], P('tm'), may hold values from -0.75 to 0.75
- local_cov: float32 [16, 2048, 2048], P('tm', 'space'), as said below
- boundary_cov: float32 [16, 2048, 2048], P('tm', 'space'), as said below
- boundary_arrow: float32 [16, 2048, 64], P('tm', 'space'), may hold values from -6 to 6
- fixed_cov: float32 [64, 64], replicated, as said below
Outputs:
- diag_blocks: float32 [16, 2048, 2048], P('tm', 'space')
- cross_blocks: float32 [16, 2048, 2048], P('tm', 'space')
- arrow_covs: float32 [16, 2048, 64], P('tm', 'space')
Inputs may be any that keep to these rules, and one draw needn't show every extreme that they name: `local_cov`: each block is symmetric. `boundary_cov`: each block is symmetric. `fixed_cov`: symmetric.
All inputs are finite; a program needn't handle non-finite values.
Results may differ from a plain program's by a relative error of at most 0.0003.
Values may be sent and summed in bfloat16 or wider, within the bound.
No kernel may reach another device: no remote copies, remote signals or barrier semaphores. Data moves between devices by JAX's collectives and lax.ppermute only.
A program may use at most 64 MiB of HBM per device.

v0:
```python
import jax
import jax.numpy as jnp
from jax import lax
from jax.sharding import PartitionSpec as P


def passed_along(block, axis, distance):
    devices = range(lax.axis_size(axis))
    route = [(i - distance, i) for i in devices if i - distance in devices]
    return lax.ppermute(block, axis, route)


def shards(coupling, arrow_link, local_cov, boundary_cov, boundary_arrow, fixed_cov):
    highest = lax.Precision.HIGHEST
    next_block, next_arrow = passed_along((boundary_cov, boundary_arrow), "tm", -1)
    panels = lax.all_gather(coupling, "space", axis=1, tiled=True)[0]
    groups = lax.axis_size("space")
    rows_here = coupling.shape[1]
    offset = lax.axis_index("space") * rows_here
    link_block = arrow_link[0]
    link_rows = lax.dynamic_slice_in_dim(link_block, offset, rows_here, 0)
    succ_rows = next_block[0]
    succ_arrow = next_arrow[0]
    gathered = lax.all_gather(succ_arrow, "space", axis=0, tiled=True)
    carried = jnp.dot(coupling[0], gathered, precision=highest, preferred_element_type=jnp.float32)
    arrow_rows = carried + jnp.dot(
        link_rows, fixed_cov, precision=highest, preferred_element_type=jnp.float32
    )
    cross_turned = jnp.dot(
        succ_rows, panels.T, precision=highest, preferred_element_type=jnp.float32
    )
    cross_turned = cross_turned + jnp.dot(
        succ_arrow, link_block.T, precision=highest, preferred_element_type=jnp.float32
    )
    pieces = (
        cross_turned.reshape(rows_here, groups, rows_here)
        .transpose(2, 1, 0)
        .reshape(rows_here, groups * rows_here)
    )
    cross_rows = lax.all_to_all(pieces, "space", split_axis=1, concat_axis=1, tiled=True)
    diag_rows = local_cov[0] + jnp.dot(
        cross_rows, panels.T, precision=highest, preferred_element_type=jnp.float32
    )
    diag_rows = diag_rows + jnp.dot(
        arrow_rows, link_block.T, precision=highest, preferred_element_type=jnp.float32
    )
    return (diag_rows[None], cross_rows[None], arrow_rows[None])


def solution(mesh):
    return jax.shard_map(
        shards,
        mesh=mesh,
        in_specs=(
            P("tm", "space", None),
            P("tm", None, None),
            P("tm", "space", None),
            P("tm", "space", None),
            P("tm", "space", None),
            P(),
        ),
        out_specs=(P("tm", "space", None), P("tm", "space", None), P("tm", "space", None)),
        check_vma=False,
    )
```

profile of v0, /device:TPU:8, one launch (start us, length us, event | category | flops | bytes accessed | tf_op | source)
XLA Modules:
  0.0 218.1 jit_solution(1109246769169374447)
XLA Ops:
  7.2 0.0 copy-start
  7.2 0.0 all-gather.3.cloned.1.call-start
  7.2 0.7 all-gather.3.cloned.1.call-update
  7.9 1.9 collective-permute-start
  9.9 7.8 %collective-permute-start.1 = (f32[1,64,64]{2,1,0:T(8,128)}, f32[1,64,64]{2,1,0:T(8,128)S(1)}, u32[]{:S(2)}, u32[]{:S(2)}) collective-permute-start(f32[1,64,64]{2,1,0:T(8,128)} %param.10), channel_id=1, source_target_pairs={{32,0},{64,32},{96,64},{128,96},{160,128},{192,160},{224,192},{256... | collective-permute-start | bytes 49160 | tf_op jit(solution)/shard_map/ppermute | solution.py:10
  17.7 1.9 collective-permute-done.1
  19.6 0.6 fusion.13
  20.2 100.1 %all-gather.3.cloned.1.call-done = bf16[1,2048,2048]{2,1,0:T(8,128)(2,1)} async-done(((bf16[1,64,2048]{2,1,0:T(8,128)(2,1)}), bf16[1,2048,2048]{2,1,0:T(8,128)(2,1)}) %all-gather.3.cloned.1.call-update) | async-done | bytes 8388624 | tf_op jit(solution)/shard_map/all_gather | solution.py:16
  120.3 10.0 %fusion.5 = f32[64,2048]{1,0:T(8,128)S(1)} fusion(f32[64,2048]{1,0:T(8,128)S(1)} %fusion.13, bf16[1,2048,2048]{2,1,0:T(8,128)(2,1)} %all-gather.3.cloned.1.call-done, f32[1,64,2048]{2,1,0:T(8,128)S(1)} %collective-permute-done), kind=kOutput, calls=%fused_computation.6 | convolution fusion | flops 3221356544 | bytes 9961472 | tf_op jit(solution)/shard_map/dot_general | solution.py:29
  130.4 0.3 copy.16
  130.7 1.5 reshape.17
  132.2 5.4 %all-to-all-start = ((f32[32,1,4096]{2,1,0:T(1,128)}), f32[32,1,4096]{2,1,0:T(1,128)S(1)}, u32[]{:S(2)}, u32[]{:S(2)}) async-start(f32[32,1,4096]{2,1,0:T(1,128)} %reshape.17), calls=%async_computation | async-start | bytes 1048576 | tf_op jit(solution)/shard_map/all_to_all | solution.py:40
  137.6 0.3 fusion.17
  138.0 56.4 %all-gather = f32[1,2048,64]{2,1,0:T(8,128)S(1)} all-gather(f32[1,64,64]{2,1,0:T(8,128)S(1)} %collective-permute-done.1), channel_id=2, replica_groups=mesh['tm'=16,'space'=32] {'space'}, dimensions={1}, use_global_device_ids=true | all-gather | bytes 540672 | tf_op jit(solution)/shard_map/all_gather | solution.py:24
  194.3 0.5 convolution_add_fusion.1
  194.8 0.0 copy-start.3
  194.8 0.5 broadcast
  195.3 1.9 reduce
  197.2 0.4 reshape.18
  197.7 0.6 copy.14
  198.3 0.4 all_to_all.7
  198.6 1.2 broadcast_in_dim.10
  199.8 10.0 %fusion.8 = f32[64,2048]{1,0:T(8,128)S(1)} fusion(f32[64,2048]{1,0:T(8,128)S(1)} %all_to_all.7, bf16[1,2048,2048]{2,1,0:T(8,128)(2,1)} %all-gather.3.cloned.1.call-done, f32[1,64,2048]{2,1,0:T(8,128)S(1)} %copy-done.2), kind=kOutput, calls=%fused_computation.7 | convolution fusion | flops 3221356544 | bytes 9961472 | tf_op jit(solution)/shard_map/dot_general | solution.py:41
  209.9 1.4 fusion.4
  (10 shorter events, 0.0 us)
Async XLA Ops:
  7.2 12.4 %copy-start = (f32[1,2048,64]{1,2,0:T(8,128)S(1)}, f32[1,2048,64]{1,2,0:T(8,128)}, u32[]{:S(2)}) copy-start(f32[1,2048,64]{1,2,0:T(8,128)} %param.7) | copy-start | bytes 1572868
  7.2 187.1 %copy-start.1 = (bf16[1,64,2048]{2,1,0:T(8,128)(2,1)S(1)}, bf16[1,64,2048]{2,1,0:T(8,128)(2,1)}, u32[]{:S(2)}) copy-start(bf16[1,64,2048]{2,1,0:T(8,128)(2,1)} %param.6) | copy-start | bytes 786436
  7.2 130.4 %copy-start.4 = (f32[64,64]{1,0:T(8,128)S(1)}, f32[64,64]{1,0:T(8,128)}, u32[]{:S(2)}) copy-start(f32[64,64]{1,0:T(8,128)} %param.11) | copy-start | bytes 49156
  7.2 113.1 %all-gather.3.cloned.1.call-start = ((), (), s32[]{:S(2)}) async-start(), calls=%async_computation.1 | async-start | bytes 8650752 | tf_op jit(solution)/shard_map/all_gather | solution.py:16
  7.9 12.2 %collective-permute-start = (f32[1,64,2048]{2,1,0:T(8,128)}, f32[1,64,2048]{2,1,0:T(8,128)S(1)}, u32[]{:S(2)}, u32[]{:S(2)}) collective-permute-start(f32[1,64,2048]{2,1,0:T(8,128)} %param.9), channel_id=1, source_target_pairs={{32,0},{64,32},{96,64},{128,96},{160,128},{192,160},{224,192},{256... | collective-permute-start | bytes 1572872 | tf_op jit(solution)/shard_map/ppermute | solution.py:10
  9.9 9.7 %collective-permute-start.1 = (f32[1,64,64]{2,1,0:T(8,128)}, f32[1,64,64]{2,1,0:T(8,128)S(1)}, u32[]{:S(2)}, u32[]{:S(2)}) collective-permute-start(f32[1,64,64]{2,1,0:T(8,128)} %param.10), channel_id=1, source_target_pairs={{32,0},{64,32},{96,64},{128,96},{160,128},{192,160},{224,192},{256... | collective-permute-start | bytes 49160 | tf_op jit(solution)/shard_map/ppermute | solution.py:10
  130.4 69.4 %copy-start.2 = (f32[1,64,2048]{2,1,0:T(8,128)S(1)}, f32[1,64,2048]{2,1,0:T(8,128)}, u32[]{:S(2)}) copy-start(f32[1,64,2048]{2,1,0:T(8,128)} %param.8) | copy-start | bytes 1572868
  132.2 62.7 %all-to-all-start = ((f32[32,1,4096]{2,1,0:T(1,128)}), f32[32,1,4096]{2,1,0:T(1,128)S(1)}, u32[]{:S(2)}, u32[]{:S(2)}) async-start(f32[32,1,4096]{2,1,0:T(1,128)} %reshape.17), calls=%async_computation | async-start | bytes 1048576 | tf_op jit(solution)/shard_map/all_to_all | solution.py:40
  194.8 15.0 %copy-start.3 = (f32[64,64]{1,0:T(8,128)}, f32[64,64]{1,0:T(8,128)S(1)}, u32[]{:S(2)}) copy-start(f32[64,64]{1,0:T(8,128)S(1)} %convolution_add_fusion.1) | copy-start | bytes 49156
Sparse Core Ops, SparseCore 0:
  11.2 109.0 all-gather.2
where the time goes:
time: 218 us
  waiting for transfers between devices  103 us (47%)
  blocking collectives  56.4 us (26%)
  matrix products  22.8 us (10%)
  starting transfers between devices  15.2 us (7%)
  between operations  14.2 us (7%)
  local copies, waits for them, and re-layouts  4.86 us (2%)
    all_gather x1, waiting for transfers between devices, shards(): panels = lax.all_gather(coupling, 'space', axis=1, tiled=True)[0]  100 us
    all_gather x1, blocking collectives, shards(): gathered = lax.all_gather(succ_arrow, 'space', axis=0, tiled=True)  56.4 us
    dot_general x1, matrix products, shards(): jnp.dot(cross_rows, panels.T, precision=highest, preferred_element_type=j...  10 us
    dot_general x1, matrix products, shards(): jnp.dot(succ_rows, panels.T, precision=highest, preferred_element_type=jn...  10 us
    ppermute x2, starting transfers between devices, passed_along(): return lax.ppermute(block, axis, route)  9.75 us
    all_to_all x1, starting transfers between devices, shards(): lax.all_to_all(pieces, 'space', split_axis=1, concat_axis=1, tiled=True)  5.45 us
  transfers between devices with their start and end apart: 4, of which 2 were waited for; matrix products, arithmetic and copies ran while one was open for 1% of the time, Pallas kernels for 0%

commit v1 on v0

--- a/solution.py
+++ b/solution.py
@@ -13,7 +13,9 @@
 def shards(coupling, arrow_link, local_cov, boundary_cov, boundary_arrow, fixed_cov):
     highest = lax.Precision.HIGHEST
     next_block, next_arrow = passed_along((boundary_cov, boundary_arrow), "tm", -1)
-    panels = lax.all_gather(coupling, "space", axis=1, tiled=True)[0]
+    panels = jnp.concatenate(
+        lax.all_to_all(jnp.stack([coupling] * lax.axis_size("space")), "space", 0, 0), axis=1
+    )[0]
     groups = lax.axis_size("space")
     rows_here = coupling.shape[1]
     offset = lax.axis_index("space") * rows_here

time: 218 us -> 308 us (1.41)
  the two profiles are of different devices: /device:TPU:8 before, /device:TPU:32 now
where the time goes in v1:
time: 308 us; the launch traced here: 307 us
  waiting for transfers between devices  184 us (60%)
  blocking collectives  55.9 us (18%)
  starting transfers between devices  31.9 us (10%)
  matrix products  22.8 us (7%)
  local copies, waits for them, and re-layouts  10.2 us (3%)
    all_to_all x1, waiting for transfers between devices, shards(): lax.all_to_all(jnp.stack([coupling] * lax.axis_size('space')), 'space', 0...  179 us
    all_gather x1, blocking collectives, shards(): gathered = lax.all_gather(succ_arrow, 'space', axis=0, tiled=True)  55.9 us
    all_to_all x1, starting transfers between devices, shards(): lax.all_to_all(pieces, 'space', split_axis=1, concat_axis=1, tiled=True)  14 us
    all_to_all x1, starting transfers between devices, shards(): lax.all_to_all(jnp.stack([coupling] * lax.axis_size('space')), 'space', 0...  13.4 us
    dot_general x1, matrix products, shards(): jnp.dot(cross_rows, panels.T, precision=highest, preferred_element_type=j...  10 us
    dot_general x1, matrix products, shards(): jnp.dot(succ_rows, panels.T, precision=highest, preferred_element_type=jn...  10 us
  transfers between devices with their start and end apart: 4, of which 2 were waited for; matrix products, arithmetic and copies ran while one was open for 0% of the time, Pallas kernels for 0%

profile of v1, /device:TPU:32, one launch (start us, length us, event | category | flops | bytes accessed | tf_op | source)
XLA Modules:
  0.0 307.2 jit_solution(16801299490468854616)
XLA Ops:
  0.6 0.0 copy-start
  0.6 5.3 %stack.2 = bf16[32,1,64,2048]{3,2,1,0:T(8,128)(2,1)} broadcast(bf16[64,2048]{1,0:T(8,128)(2,1)} %bitcast.38), dimensions={2,3} | broadcast | bytes 8650752 | tf_op jit(solution)/shard_map/stack | solution.py:17
  6.0 13.4 %all-to-all-start = ((bf16[32,1,64,2048]{3,2,1,0:T(8,128)(2,1)}), bf16[32,1,64,2048]{3,2,1,0:T(8,128)(2,1)}, u32[]{:S(2)}, u32[]{:S(2)}) async-start(bf16[32,1,64,2048]{3,2,1,0:T(8,128)(2,1)} %stack.2), calls=%async_computation | async-start | bytes 16777216 | tf_op jit(solution)/shard_map/all_to_all | solution.py:17
  19.4 2.1 collective-permute-start
  21.5 2.5 collective-permute-start.1
  24.0 4.5 %collective-permute-done.1 = f32[1,64,64]{2,1,0:T(8,128)S(1)} collective-permute-done((f32[1,64,64]{2,1,0:T(8,128)S(1)}, f32[1,64,64]{2,1,0:T(8,128)S(1)}, u32[]{:S(2)}, u32[]{:S(2)}) %collective-permute-start.1) | collective-permute-done | bytes 16416 | tf_op jit(solution)/shard_map/ppermute | solution.py:10
  28.5 0.6 fusion.3
  29.1 179.1 %all-to-all-done = bf16[32,1,64,2048]{3,2,1,0:T(8,128)(2,1)} async-done(((bf16[32,1,64,2048]{3,2,1,0:T(8,128)(2,1)}), bf16[32,1,64,2048]{3,2,1,0:T(8,128)(2,1)}, u32[]{:S(2)}, u32[]{:S(2)}) %all-to-all-start) | async-done | bytes 8388640 | tf_op jit(solution)/shard_map/all_to_all | solution.py:17
  208.2 10.0 %convolution_add_fusion.2 = f32[64,2048]{1,0:T(8,128)S(1)} fusion(f32[64,2048]{1,0:T(8,128)S(1)} %fusion.3, bf16[2048,2048]{1,0:T(8,128)(2,1)} %bitcast.3, f32[1,64,2048]{2,1,0:T(8,128)S(1)} %collective-permute-done), kind=kOutput, calls=%fused_computation.2 | convolution fusion | flops 3221356544 | bytes 9961472 | tf_op jit(solution)/shard_map/dot_general | solution.py:31
  218.2 0.3 copy.16
  218.6 1.5 reshape.20
  220.0 14.0 %all-to-all-start.1 = ((f32[32,1,4096]{2,1,0:T(1,128)}), f32[32,1,4096]{2,1,0:T(1,128)S(1)}, u32[]{:S(2)}, u32[]{:S(2)}) async-start(f32[32,1,4096]{2,1,0:T(1,128)} %reshape.20), calls=%async_computation.1 | async-start | bytes 1048576 | tf_op jit(solution)/shard_map/all_to_all | solution.py:42
  234.0 0.3 fusion.6
  234.3 55.9 %all-gather = f32[1,2048,64]{2,1,0:T(8,128)S(1)} all-gather(f32[1,64,64]{2,1,0:T(8,128)S(1)} %collective-permute-done.1), channel_id=2, replica_groups=mesh['tm'=16,'space'=32] {'space'}, dimensions={1}, use_global_device_ids=true | all-gather | bytes 540672 | tf_op jit(solution)/shard_map/all_gather | solution.py:26
  290.3 0.5 convolution_add_fusion.3
  290.8 0.0 copy-start.3
  290.8 0.5 broadcast.3
  291.3 1.9 reduce
  293.2 0.4 reshape.21
  293.6 0.6 copy.14
  294.3 0.4 all_to_all.11
  294.6 1.2 broadcast_in_dim.10
  295.8 10.0 %convolution_add_fusion.1 = f32[64,2048]{1,0:T(8,128)S(1)} fusion(f32[64,2048]{1,0:T(8,128)S(1)} %all_to_all.11, bf16[2048,2048]{1,0:T(8,128)(2,1)} %bitcast.3, f32[1,64,2048]{2,1,0:T(8,128)S(1)} %copy-done.2), kind=kOutput, calls=%fused_computation.1 | convolution fusion | flops 3221356544 | bytes 9961472 | tf_op jit(solution)/shard_map/dot_general | solution.py:43
  305.8 1.4 fusion
  (14 shorter events, 0.0 us)
Async XLA Ops:
  0.6 27.9 %copy-start = (f32[1,2048,64]{1,2,0:T(8,128)S(1)}, f32[1,2048,64]{1,2,0:T(8,128)}, u32[]{:S(2)}) copy-start(f32[1,2048,64]{1,2,0:T(8,128)} %param.7) | copy-start | bytes 1572868
  6.0 13.4 %copy-start.5 = (f32[1,64,2048]{2,1,0:T(8,128)S(1)}, f32[1,64,2048]{2,1,0:T(8,128)}, u32[]{:S(2)}) copy-start(f32[1,64,2048]{2,1,0:T(8,128)} %param.9) | copy-start | bytes 1572868
  6.0 15.5 %copy-start.6 = (f32[1,64,64]{2,1,0:T(8,128)S(1)}, f32[1,64,64]{2,1,0:T(8,128)}, u32[]{:S(2)}) copy-start(f32[1,64,64]{2,1,0:T(8,128)} %param.10) | copy-start | bytes 49156
  6.0 202.2 %all-to-all-start = ((bf16[32,1,64,2048]{3,2,1,0:T(8,128)(2,1)}), bf16[32,1,64,2048]{3,2,1,0:T(8,128)(2,1)}, u32[]{:S(2)}, u32[]{:S(2)}) async-start(bf16[32,1,64,2048]{3,2,1,0:T(8,128)(2,1)} %stack.2), calls=%async_computation | async-start | bytes 16777216 | tf_op jit(solution)/shard_map/all_to_all | solution.py:17
  19.4 214.6 %copy-start.4 = (f32[64,64]{1,0:T(8,128)S(1)}, f32[64,64]{1,0:T(8,128)}, u32[]{:S(2)}) copy-start(f32[64,64]{1,0:T(8,128)} %param.11) | copy-start | bytes 49156
  19.4 270.9 %copy-start.1 = (bf16[1,64,2048]{2,1,0:T(8,128)(2,1)S(1)}, bf16[1,64,2048]{2,1,0:T(8,128)(2,1)}, u32[]{:S(2)}) copy-start(bf16[1,64,2048]{2,1,0:T(8,128)(2,1)} %param.6) | copy-start | bytes 786436
  19.4 9.7 %collective-permute-start = (f32[1,64,2048]{2,1,0:T(8,128)S(1)}, f32[1,64,2048]{2,1,0:T(8,128)S(1)}, u32[]{:S(2)}, u32[]{:S(2)}) collective-permute-start(f32[1,64,2048]{2,1,0:T(8,128)S(1)} %copy-done.5), channel_id=1, source_target_pairs={{32,0},{64,32},{96,64},{128,96},{160,128},{192,160},{224,192},{256... | collective-permute-start | bytes 1572872 | tf_op jit(solution)/shard_map/ppermute | solution.py:10
  21.5 7.0 %collective-permute-start.1 = (f32[1,64,64]{2,1,0:T(8,128)S(1)}, f32[1,64,64]{2,1,0:T(8,128)S(1)}, u32[]{:S(2)}, u32[]{:S(2)}) collective-permute-start(f32[1,64,64]{2,1,0:T(8,128)S(1)} %copy-done.6), channel_id=1, source_target_pairs={{32,0},{64,32},{96,64},{128,96},{160,128},{192,160},{224,192},{256... | collective-permute-start | bytes 49160 | tf_op jit(solution)/shard_map/ppermute | solution.py:10
  218.2 77.5 %copy-start.2 = (f32[1,64,2048]{2,1,0:T(8,128)S(1)}, f32[1,64,2048]{2,1,0:T(8,128)}, u32[]{:S(2)}) copy-start(f32[1,64,2048]{2,1,0:T(8,128)} %param.8) | copy-start | bytes 1572868
  220.0 70.8 %all-to-all-start.1 = ((f32[32,1,4096]{2,1,0:T(1,128)}), f32[32,1,4096]{2,1,0:T(1,128)S(1)}, u32[]{:S(2)}, u32[]{:S(2)}) async-start(f32[32,1,4096]{2,1,0:T(1,128)} %reshape.20), calls=%async_computation.1 | async-start | bytes 1048576 | tf_op jit(solution)/shard_map/all_to_all | solution.py:42
  290.8 15.0 %copy-start.3 = (f32[64,64]{1,0:T(8,128)}, f32[64,64]{1,0:T(8,128)S(1)}, u32[]{:S(2)}) copy-start(f32[64,64]{1,0:T(8,128)S(1)} %convolution_add_fusion.3) | copy-start | bytes 49156

commit v2 on v0

--- a/solution.py
+++ b/solution.py
@@ -37,7 +37,10 @@
         .transpose(2, 1, 0)
         .reshape(rows_here, groups * rows_here)
     )
-    cross_rows = lax.all_to_all(pieces, "space", split_axis=1, concat_axis=1, tiled=True)
+    cross_rows = jnp.concatenate(
+        lax.all_to_all(jnp.stack(jnp.split(pieces, lax.axis_size("space"), axis=1)), "space", 0, 0),
+        axis=1,
+    )
     diag_rows = local_cov[0] + jnp.dot(
         cross_rows, panels.T, precision=highest, preferred_element_type=jnp.float32
     )

time: 218 us -> 221 us (1.014)
  local copies, waits for them, and re-layouts: 4.86 us -> 7.68 us
where the time goes in v2:
time: 221 us
  waiting for transfers between devices  103 us (47%)
  blocking collectives  56.4 us (26%)
  matrix products  22.8 us (10%)
  starting transfers between devices  15.2 us (7%)
  between operations  14.3 us (6%)
  local copies, waits for them, and re-layouts  7.68 us (3%)
    all_gather x1, waiting for transfers between devices, shards(): panels = lax.all_gather(coupling, 'space', axis=1, tiled=True)[0]  100 us
    all_gather x1, blocking collectives, shards(): gathered = lax.all_gather(succ_arrow, 'space', axis=0, tiled=True)  56.4 us
    dot_general x1, matrix products, shards(): jnp.dot(cross_rows, panels.T, precision=highest, preferred_element_type=j...  10 us
    dot_general x1, matrix products, shards(): jnp.dot(succ_rows, panels.T, precision=highest, preferred_element_type=jn...  10 us
    ppermute x2, starting transfers between devices, passed_along(): return lax.ppermute(block, axis, route)  9.75 us
    all_to_all x1, starting transfers between devices, shards(): lax.all_to_all(jnp.stack(jnp.split(pieces, lax.axis_size('space'), axis=1...  5.44 us
  transfers between devices with their start and end apart: 4, of which 2 were waited for; matrix products, arithmetic and copies ran while one was open for 1% of the time, Pallas kernels for 0%

profile of v2, /device:TPU:8, one launch (start us, length us, event | category | flops | bytes accessed | tf_op | source)
XLA Modules:
  0.0 221.0 jit_solution(16883251507901689929)
XLA Ops:
  7.2 0.7 all-gather.3.cloned.1.call-update
  7.9 1.9 collective-permute-start
  9.8 7.8 %collective-permute-start.1 = (f32[1,64,64]{2,1,0:T(8,128)}, f32[1,64,64]{2,1,0:T(8,128)S(1)}, u32[]{:S(2)}, u32[]{:S(2)}) collective-permute-start(f32[1,64,64]{2,1,0:T(8,128)} %param.10), channel_id=1, source_target_pairs={{32,0},{64,32},{96,64},{128,96},{160,128},{192,160},{224,192},{256... | collective-permute-start | bytes 49160 | tf_op jit(solution)/shard_map/ppermute | solution.py:10
  17.7 1.9 collective-permute-done.1
  19.6 0.6 fusion.13
  20.2 100.1 %all-gather.3.cloned.1.call-done = bf16[1,2048,2048]{2,1,0:T(8,128)(2,1)} async-done(((bf16[1,64,2048]{2,1,0:T(8,128)(2,1)}), bf16[1,2048,2048]{2,1,0:T(8,128)(2,1)}) %all-gather.3.cloned.1.call-update) | async-done | bytes 8388624 | tf_op jit(solution)/shard_map/all_gather | solution.py:16
  120.3 10.0 %fusion.5 = f32[64,2048]{1,0:T(8,128)S(1)} fusion(f32[64,2048]{1,0:T(8,128)S(1)} %fusion.13, bf16[1,2048,2048]{2,1,0:T(8,128)(2,1)} %all-gather.3.cloned.1.call-done, f32[1,64,2048]{2,1,0:T(8,128)S(1)} %collective-permute-done), kind=kOutput, calls=%fused_computation.6 | convolution fusion | flops 3221356544 | bytes 9961472 | tf_op jit(solution)/shard_map/dot_general | solution.py:29
  130.3 0.4 reshape.19
  130.8 1.1 copy.41
  131.9 0.4 reshape.20
  132.2 0.1 constant_dynamic-update-slice_fusion.30
  133.6 1.4 reshape.24
  135.0 5.4 %all-to-all-start = ((f32[32,1,4096]{2,1,0:T(1,128)}), f32[32,1,4096]{2,1,0:T(1,128)S(1)}, u32[]{:S(2)}, u32[]{:S(2)}) async-start(f32[32,1,4096]{2,1,0:T(1,128)} %reshape.24), calls=%async_computation | async-start | bytes 1048576 | tf_op jit(solution)/shard_map/all_to_all | solution.py:41
  140.5 0.3 fusion.17
  140.8 56.4 %all-gather = f32[1,2048,64]{2,1,0:T(8,128)S(1)} all-gather(f32[1,64,64]{2,1,0:T(8,128)S(1)} %collective-permute-done.1), channel_id=2, replica_groups=mesh['tm'=16,'space'=32] {'space'}, dimensions={1}, use_global_device_ids=true | all-gather | bytes 540672 | tf_op jit(solution)/shard_map/all_gather | solution.py:24
  197.2 0.5 convolution_add_fusion.1
  197.7 0.5 broadcast
  198.2 1.9 reduce
  200.1 0.4 reshape.25
  200.5 0.6 copy.42
  201.2 0.4 reshape.22
  201.5 1.2 broadcast_in_dim_reshape.3
  202.7 10.0 %fusion.8 = f32[64,2048]{1,0:T(8,128)S(1)} fusion(f32[64,2048]{1,0:T(8,128)S(1)} %reshape.22, bf16[1,2048,2048]{2,1,0:T(8,128)(2,1)} %all-gather.3.cloned.1.call-done, f32[1,64,2048]{2,1,0:T(8,128)S(1)} %copy-done.2), kind=kOutput, calls=%fused_computation.7 | convolution fusion | flops 3221356544 | bytes 9961472 | tf_op jit(solution)/shard_map/dot_general | solution.py:44
  212.7 1.4 fusion.4
  (44 shorter events, 1.3 us)
Async XLA Ops:
  7.2 12.4 %copy-start = (f32[1,2048,64]{1,2,0:T(8,128)S(1)}, f32[1,2048,64]{1,2,0:T(8,128)}, u32[]{:S(2)}) copy-start(f32[1,2048,64]{1,2,0:T(8,128)} %param.7) | copy-start | bytes 1572868
  7.2 113.1 %all-gather.3.cloned.1.call-start = ((), (), s32[]{:S(2)}) async-start(), calls=%async_computation.1 | async-start | bytes 8650752 | tf_op jit(solution)/shard_map/all_gather | solution.py:16
  7.9 12.3 %collective-permute-start = (f32[1,64,2048]{2,1,0:T(8,128)}, f32[1,64,2048]{2,1,0:T(8,128)S(1)}, u32[]{:S(2)}, u32[]{:S(2)}) collective-permute-start(f32[1,64,2048]{2,1,0:T(8,128)} %param.9), channel_id=1, source_target_pairs={{32,0},{64,32},{96,64},{128,96},{160,128},{192,160},{224,192},{256... | collective-permute-start | bytes 1572872 | tf_op jit(solution)/shard_map/ppermute | solution.py:10
  9.8 9.7 %collective-permute-start.1 = (f32[1,64,64]{2,1,0:T(8,128)}, f32[1,64,64]{2,1,0:T(8,128)S(1)}, u32[]{:S(2)}, u32[]{:S(2)}) collective-permute-start(f32[1,64,64]{2,1,0:T(8,128)} %param.10), channel_id=1, source_target_pairs={{32,0},{64,32},{96,64},{128,96},{160,128},{192,160},{224,192},{256... | collective-permute-start | bytes 49160 | tf_op jit(solution)/shard_map/ppermute | solution.py:10
  20.2 120.3 %copy-start.4 = (f32[64,64]{1,0:T(8,128)S(1)}, f32[64,64]{1,0:T(8,128)}, u32[]{:S(2)}) copy-start(f32[64,64]{1,0:T(8,128)} %param.11) | copy-start | bytes 49156
  20.2 177.0 %copy-start.1 = (bf16[1,64,2048]{2,1,0:T(8,128)(2,1)S(1)}, bf16[1,64,2048]{2,1,0:T(8,128)(2,1)}, u32[]{:S(2)}) copy-start(bf16[1,64,2048]{2,1,0:T(8,128)(2,1)} %param.6) | copy-start | bytes 786436
  131.9 70.8 %copy-start.2 = (f32[1,64,2048]{2,1,0:T(8,128)S(1)}, f32[1,64,2048]{2,1,0:T(8,128)}, u32[]{:S(2)}) copy-start(f32[1,64,2048]{2,1,0:T(8,128)} %param.8) | copy-start | bytes 1572868
  135.0 62.6 %all-to-all-start = ((f32[32,1,4096]{2,1,0:T(1,128)}), f32[32,1,4096]{2,1,0:T(1,128)S(1)}, u32[]{:S(2)}, u32[]{:S(2)}) async-start(f32[32,1,4096]{2,1,0:T(1,128)} %reshape.24), calls=%async_computation | async-start | bytes 1048576 | tf_op jit(solution)/shard_map/all_to_all | solution.py:41
  197.7 15.0 %copy-start.3 = (f32[64,64]{1,0:T(8,128)}, f32[64,64]{1,0:T(8,128)S(1)}, u32[]{:S(2)}) copy-start(f32[64,64]{1,0:T(8,128)S(1)} %convolution_add_fusion.1) | copy-start | bytes 49156
Sparse Core Ops, SparseCore 0:
  11.2 109.0 all-gather.2
